TPU v7x, 32 devices: a whole 2x2x4 slice. The times are simulated.
32 devices in a mesh: tm: 4 (over x, core), port: 8 (over z, y).
Axes of the slice: x: 2, y: 2, z: 4, core: 2. Of those that a mesh axis runs over, the one named last changes fastest.
Arguments:
- counters: bfloat16 [4096, 256], P('tm'), may hold values from -6 to 6
- signatures: bfloat16 [256, 8192], P(None, 'port'), may hold values from -0.375 to 0.375
- eigen_vectors_at_pins: bfloat16 [8192, 256], P('port'), may hold values from -0.09375 to 0.09375
- taps: bfloat16 [256, 4096], P('port'), may hold values from -0.5 to 0.5
Outputs:
- voltage_sag: bfloat16 [4096, 8192], P('tm', 'port')
All inputs are finite; a program needn't handle non-finite values.
Results may differ from a plain program's by a relative error of at most 0.007.
Values may be sent and summed in bfloat16 or wider, within the bound.
A program may use at most 192 MiB of HBM per device.

v0:
```python
import functools

import jax
import jax.numpy as jnp
import ml_dtypes
import numpy as np
from jax import lax
from jax.experimental import pallas as pl
from jax.experimental.pallas import tpu as pltpu
from jax.sharding import PartitionSpec as P

MESH = pl.DeviceIdType.MESH
F32 = jnp.float32
BF16 = jnp.bfloat16
NT = (((1,), (1,)), ((), ()))
TN = (((0,), (0,)), ((), ()))


def split_parts(x):
    high = x.astype(ml_dtypes.bfloat16)
    low = (x - high.astype(np.float64)).astype(ml_dtypes.bfloat16)
    return high, low


def odd_dft(width):
    theta = np.pi * (2 * np.arange(width) + 1) / (2 * width)
    phase = np.outer(np.arange(width), theta)
    forward = np.concatenate([np.cos(phase), -np.sin(phase)], axis=1)
    phase = np.outer(theta, width + np.arange(width))
    inverse = np.concatenate([np.cos(phase), -np.sin(phase)], axis=0) / width
    return np.concatenate(split_parts(forward), axis=0), np.concatenate(split_parts(inverse), axis=0)


def halves(x):
    high = x.astype(BF16)
    return high, (x - high.astype(F32)).astype(BF16)


def dot(a, b):
    return jnp.dot(a, b, preferred_element_type=F32)


class Plan:
    def __init__(self, tm, port, cycles, ports, tallies, own, span):
        self.tm, self.port, self.cycles, self.ports, self.tallies = tm, port, cycles, ports, tallies
        self.own, self.span = own, span
        self.width = min(256, cycles)
        self.blocks = cycles // self.width
        self.lags = span // self.width
        self.reach = min((span - 2) // cycles + 1, tm - 1)
        self.ways = min(tm, own // 8)
        self.line = port // 2


def response_kernel(
    plan, counters, signatures, eigen, taps, forward, inverse, out,
    cnt, sig, eig, tap, fwd, inv, partial, parts, merged, xs, spectra, taps_spectra, product,
    load_sem, part_send, part_recv, merged_send, merged_recv, modal_send, modal_recv, out_send, out_recv,
):
    T, N, W, C, R, own = plan.tm, plan.port, plan.width, plan.blocks, plan.reach, plan.own
    t, p = lax.axis_index("tm"), lax.axis_index("port")
    loads = [
        pltpu.make_async_copy(src, dst, load_sem.at[i])
        for i, (src, dst) in enumerate(
            [(signatures, sig), (eigen, eig), (forward, fwd), (taps, tap), (counters, cnt), (inverse, inv)]
        )
    ]
    for load in loads:
        load.start()

    barrier = pltpu.get_barrier_semaphore()
    for k in range(1, N):
        pl.semaphore_signal(
            barrier, inc=1, device_id={"tm": t, "port": lax.rem(p + k, N)}, device_id_type=MESH
        )
    greeted = N - 1
    for k in range(1, R + 1):
        @pl.when(t + k < T)
        def _():
            pl.semaphore_signal(barrier, inc=1, device_id={"tm": t + k, "port": p}, device_id_type=MESH)

        @pl.when(t - k >= 0)
        def _():
            pl.semaphore_signal(barrier, inc=1, device_id={"tm": t - k, "port": p}, device_id_type=MESH)

        greeted = greeted + jnp.where(t + k < T, 1, 0) + jnp.where(t - k >= 0, 1, 0)

    loads[0].wait()
    loads[1].wait()
    partial[...] = dot(sig[...], eig[...]).T
    pl.semaphore_wait(barrier, greeted)

    share = lax.rem(t, plan.ways)

    def part_copy(k):
        to = lax.rem(p + k, N)
        return pltpu.make_async_remote_copy(
            src_ref=partial.at[pl.ds(pl.multiple_of(to * own + share * 8, 8), 8)],
            dst_ref=parts.at[k],
            send_sem=part_send.at[k],
            recv_sem=part_recv.at[k],
            device_id={"tm": t, "port": to},
            device_id_type=MESH,
        )

    for k in range(1, N):
        part_copy(k).start()

    loads[2].wait()
    loads[3].wait()

    def transform(x):
        return dot(x, fwd[:W]) + dot(x, fwd[W:])

    quad = 4

    def taps_step(i, carry):
        rows = [
            tap[:, pl.ds(pl.multiple_of((i * quad + j) * W, W), W)] for j in range(quad)
        ]
        result = transform(jnp.concatenate(rows, axis=0))
        taps_spectra[pl.ds(i * quad, quad)] = result.reshape(quad, own, 2 * W)
        return carry

    lax.fori_loop(0, plan.lags // quad, taps_step, 0)
    for d in range(1, R + 1):
        @pl.when(t < d)
        def _():
            xs[d] = jnp.zeros_like(xs[d])

    total = partial[pl.ds(pl.multiple_of(p * own + share * 8, 8), 8)]
    for k in range(1, N):
        part_copy(k).wait_recv()
        total = total + parts[k]
    merged[share] = total

    def merged_copy(k):
        mate = t - share + lax.rem(share + k, plan.ways)
        return pltpu.make_async_remote_copy(
            src_ref=merged.at[share],
            dst_ref=merged.at[share],
            send_sem=merged_send.at[k],
            recv_sem=merged_recv.at[k],
            device_id={"tm": mate, "port": p},
            device_id_type=MESH,
        )

    for k in range(1, plan.ways):
        merged_copy(k).start()
    loads[4].wait()
    for k in range(1, plan.ways):
        came = lax.rem(share + plan.ways - k, plan.ways)
        pltpu.make_async_remote_copy(
            src_ref=merged.at[came], dst_ref=merged.at[came], send_sem=merged_send.at[k],
            recv_sem=merged_recv.at[k], device_id={"tm": t - share + came, "port": p}, device_id_type=MESH,
        ).wait_recv()

    high, low = halves(merged[...].reshape(own, plan.tallies))
    both = lax.dot_general(jnp.concatenate([high, low], axis=0), cnt[...], NT, preferred_element_type=F32)
    xs[0] = (both[:own] + both[own:]).astype(BF16)

    def modal_copy(d):
        return pltpu.make_async_remote_copy(
            src_ref=xs.at[0],
            dst_ref=xs.at[d],
            send_sem=modal_send.at[d],
            recv_sem=modal_recv.at[d],
            device_id={"tm": t + d, "port": p},
            device_id_type=MESH,
        )

    for d in range(1, R + 1):
        @pl.when(t + d < T)
        def _():
            modal_copy(d).start()

    def spectra_of(d):
        rows = jnp.concatenate([xs[d, :, i * W : (i + 1) * W] for i in range(C)], axis=0)
        spectra[(R - d) * C : (R - d + 1) * C] = transform(rows).reshape(C, own, 2 * W)

    spectra_of(0)
    for d in range(1, R + 1):
        @pl.when(t >= d)
        def _():
            modal_copy(d).wait_recv()

        spectra_of(d)

    sign = 1.0 - 2.0 * (lax.broadcasted_iota(jnp.int32, (8, 128), 1) % 2).astype(F32)

    def product_step(g, carry):
        rows = pl.ds(pl.multiple_of(g * 8, 8), 8)
        for q in range(W // 128):
            re, im = slice(q * 128, q * 128 + 128), slice(W + q * 128, W + q * 128 + 128)
            acc_re, acc_im = [None] * C, [None] * C
            before = None
            for j in range(-R * C, C):
                now = (spectra[R * C + j, rows, re], spectra[R * C + j, rows, im])
                z_re, z_im = sign * now[1], -(sign * now[0])
                if before is not None:
                    z_re, z_im = z_re + before[0], z_im + before[1]
                before = now
                for a in range(C):
                    lag = a - j
                    if 0 <= lag < plan.lags:
                        h_re, h_im = taps_spectra[lag, rows, re], taps_spectra[lag, rows, im]
                        add_re, add_im = h_re * z_re - h_im * z_im, h_re * z_im + h_im * z_re
                        acc_re[a] = add_re if acc_re[a] is None else acc_re[a] + add_re
                        acc_im[a] = add_im if acc_im[a] is None else acc_im[a] + add_im
            for a in range(C):
                product[a, rows, re] = acc_re[a]
                product[a, rows, im] = acc_im[a]
        return carry

    lax.fori_loop(0, own // 8, product_step, 0)
    loads[5].wait()
    high, low = halves(product[...].reshape(C * own, 2 * W))
    result = dot(high, inv[: 2 * W]) + dot(low, inv[: 2 * W]) + dot(high, inv[2 * W :])
    out[p] = result.astype(BF16).reshape(C, own, W)

    place, side = p // 2, lax.rem(p, 2)

    def out_copy(piece, c, way, to):
        return pltpu.make_async_remote_copy(
            src_ref=out.at[piece, c],
            dst_ref=out.at[piece, c],
            send_sem=out_send.at[piece, c, way],
            recv_sem=out_recv.at[piece, c],
            device_id={"tm": t, "port": to},
            device_id_type=MESH,
        )

    up, down, partner = 0, 1, 2
    mate = p + 1 - 2 * side

    def send_own(c, carry):
        @pl.when(place + 1 < plan.line)
        def _():
            out_copy(p, c, up, p + 2).start()

        @pl.when(place >= 1)
        def _():
            out_copy(p, c, down, p - 2).start()

        out_copy(p, c, partner, mate).start()
        return carry

    lax.fori_loop(0, C, send_own, 0)
    for k in range(1, plan.line):
        def forward_step(c, carry):
            @pl.when(place >= k)
            def _():
                piece = p - 2 * k
                out_copy(piece, c, up, p).wait_recv()

                @pl.when(place + 1 < plan.line)
                def _():
                    out_copy(piece, c, up, p + 2).start()

                out_copy(piece, c, partner, mate).start()

            @pl.when(place + k < plan.line)
            def _():
                piece = p + 2 * k
                out_copy(piece, c, down, p).wait_recv()

                @pl.when(place >= 1)
                def _():
                    out_copy(piece, c, down, p - 2).start()

                out_copy(piece, c, partner, mate).start()

            return carry

        lax.fori_loop(0, C, forward_step, 0)

    def finish(i, carry):
        c = lax.rem(i, C)
        z = i // C
        out_copy(2 * z + 1 - side, c, partner, mate).wait_recv()
        piece = 2 * z + side
        out_copy(piece, c, partner, mate).wait_send()

        @pl.when((z <= place) & (place + 1 < plan.line))
        def _():
            out_copy(piece, c, up, p).wait_send()

        @pl.when((z >= place) & (place >= 1))
        def _():
            out_copy(piece, c, down, p).wait_send()

        return carry

    lax.fori_loop(0, plan.line * C, finish, 0)
    for k in range(1, N):
        part_copy(k).wait_send()
    for k in range(1, plan.ways):
        merged_copy(k).wait_send()
    for d in range(1, R + 1):
        @pl.when(t + d < T)
        def _():
            modal_copy(d).wait_send()


def response_call(plan, counters, signatures, eigen, taps, forward, inverse):
    T, N, W, C, R, own = plan.tm, plan.port, plan.width, plan.blocks, plan.reach, plan.own
    dma = pltpu.SemaphoreType.DMA
    return pl.pallas_call(
        functools.partial(response_kernel, plan),
        out_shape=jax.ShapeDtypeStruct((N, C, own, W), BF16),
        in_specs=[pl.BlockSpec(memory_space=pl.ANY)] * 6,
        out_specs=pl.BlockSpec(memory_space=pltpu.VMEM),
        scratch_shapes=[
            pltpu.VMEM(counters.shape, BF16),
            pltpu.VMEM(signatures.shape, BF16),
            pltpu.VMEM(eigen.shape, BF16),
            pltpu.VMEM(taps.shape, BF16),
            pltpu.VMEM(forward.shape, BF16),
            pltpu.VMEM(inverse.shape, BF16),
            pltpu.VMEM((N * own, plan.tallies), F32),
            pltpu.VMEM((N, 8, plan.tallies), F32),
            pltpu.VMEM((plan.ways, 8, plan.tallies), F32),
            pltpu.VMEM((R + 1, own, plan.cycles), BF16),
            pltpu.VMEM(((R + 1) * C, own, 2 * W), F32),
            pltpu.VMEM((plan.lags, own, 2 * W), F32),
            pltpu.VMEM((C, own, 2 * W), F32),
            dma((6,)), dma((N,)), dma((N,)), dma((plan.ways,)), dma((plan.ways,)),
            dma((R + 1,)), dma((R + 1,)), dma((N, C, 3)), dma((N, C)),
        ],
        compiler_params=pltpu.CompilerParams(
            collective_id=0, has_side_effects=True, vmem_limit_bytes=32 * 1024 * 1024
        ),
        name="response",
    )(counters, signatures, eigen, taps, forward, inverse)


def output_kernel(plan, response, eigen, out):
    block = response[...].reshape(plan.port * plan.own, plan.width)
    turned = block.T
    out[...] = lax.dot_general(turned, eigen[...], NT, preferred_element_type=F32).astype(BF16)


def output_call(plan, response, eigen):
    return pl.pallas_call(
        functools.partial(output_kernel, plan),
        grid=(plan.blocks,),
        out_shape=jax.ShapeDtypeStruct((plan.cycles, plan.ports), BF16),
        in_specs=[
            pl.BlockSpec((plan.port, None, plan.own, plan.width), lambda a: (0, a, 0, 0)),
            pl.BlockSpec(eigen.shape, lambda a: (0, 0)),
        ],
        out_specs=pl.BlockSpec((plan.width, plan.ports), lambda a: (a, 0)),
        compiler_params=pltpu.CompilerParams(vmem_limit_bytes=24 * 1024 * 1024),
        name="output",
    )(response, eigen)


def solution(mesh):
    def per_device(counters, signatures, eigen, taps):
        plan = Plan(
            mesh.shape["tm"], mesh.shape["port"], counters.shape[0], eigen.shape[0],
            counters.shape[1], taps.shape[0], taps.shape[1],
        )
        forward, inverse = odd_dft(plan.width)
        response = response_call(
            plan, counters, signatures, eigen, taps, jnp.asarray(forward), jnp.asarray(inverse)
        )
        return output_call(plan, response, eigen)

    in_specs = (P("tm", None), P(None, "port"), P("port", None), P("port", None))
    return jax.shard_map(
        per_device, mesh=mesh, in_specs=in_specs, out_specs=P("tm", "port"), check_vma=False
    )
```

profile of v0, /device:TPU:2, one launch (start us, length us, event | category | flops | bytes accessed | tf_op | source)
XLA Modules:
  0.0 39.8 jit_solution(7562562082774818036)
XLA Ops:
  0.0 0.0 copy-start
  0.0 1.0 %copy-done = bf16[1024,256]{1,0:T(8,128)(2,1)S(1)} copy-done((bf16[1024,256]{1,0:T(8,128)(2,1)S(1)}, bf16[1024,256]{1,0:T(8,128)(2,1)}, u32[]{:S(2)}) %copy-start) | copy-done | bytes 524312
  1.0 0.0 copy-start.1
  1.0 1.0 %copy-done.1 = bf16[1024,256]{1,0:T(8,128)(2,1)S(1)} copy-done((bf16[1024,256]{1,0:T(8,128)(2,1)S(1)}, bf16[1024,256]{1,0:T(8,128)(2,1)}, u32[]{:S(2)}) %copy-start.1) | copy-done | bytes 524312
  2.1 0.0 copy-start.2
  2.1 1.0 %copy-done.2 = bf16[256,1024]{1,0:T(8,128)(2,1)S(1)} copy-done((bf16[256,1024]{1,0:T(8,128)(2,1)S(1)}, bf16[256,1024]{1,0:T(8,128)(2,1)}, u32[]{:S(2)}) %copy-start.2) | copy-done | bytes 524312
  3.1 0.0 copy-start.3
  3.1 1.0 %copy-done.3 = bf16[1024,256]{1,0:T(8,128)(2,1)S(1)} copy-done((bf16[1024,256]{1,0:T(8,128)(2,1)S(1)}, bf16[1024,256]{1,0:T(8,128)(2,1)}, u32[]{:S(2)}) %copy-start.3) | copy-done | bytes 524312
  4.2 0.0 copy-start.4
  4.2 1.0 %copy-done.4 = bf16[512,512]{1,0:T(8,128)(2,1)S(1)} copy-done((bf16[512,512]{1,0:T(8,128)(2,1)S(1)}, bf16[512,512]{1,0:T(8,128)(2,1)}, u32[]{:S(2)}) %copy-start.4) | copy-done | bytes 524312
  5.2 0.0 copy-start.5
  5.2 0.9 %copy-done.5 = bf16[32,4096]{1,0:T(8,128)(2,1)S(1)} copy-done((bf16[32,4096]{1,0:T(8,128)(2,1)S(1)}, bf16[32,4096]{1,0:T(8,128)(2,1)}, u32[]{:S(2)}) %copy-start.5) | copy-done | bytes 262168
  6.2 30.9 %response.1 = bf16[8,4,32,256]{3,2,1,0:T(8,128)(2,1)S(1)} custom-call(bf16[1024,256]{1,0:T(8,128)(2,1)S(1)} %copy-done.1, bf16[256,1024]{1,0:T(8,128)(2,1)S(1)} %copy-done.2, bf16[1024,256]{1,0:T(8,128)(2,1)S(1)} %copy-done, bf16[32,4096]{1,0:T(8,128)(2,1)S(1)} %copy-done.5, bf16[512,512]{1,0:T(8,128)(2,1)S(1)} %copy-done.4, bf16[1024,256]{1,0:T(8,128)(2,1)S(1)} %copy-done.3), custom_call_target="tpu_custom_call" | custom-call | tf_op jit(solution)/shard_map/response/pallas_call | solution.py:308
  37.1 2.7 %output.1 = bf16[1024,1024]{1,0:T(8,128)(2,1)} custom-call(bf16[8,4,32,256]{3,2,1,0:T(8,128)(2,1)S(1)} %response.1, bf16[1024,256]{1,0:T(8,128)(2,1)S(1)} %copy-done), custom_call_target="tpu_custom_call" | custom-call | tf_op jit(solution)/shard_map/output/pallas_call | solution.py:344
Async XLA Ops:
  0.0 1.0 %copy-start = (bf16[1024,256]{1,0:T(8,128)(2,1)S(1)}, bf16[1024,256]{1,0:T(8,128)(2,1)}, u32[]{:S(2)}) copy-start(bf16[1024,256]{1,0:T(8,128)(2,1)} %eigen.3) | copy-start | bytes 1572868
  1.0 1.0 %copy-start.1 = (bf16[1024,256]{1,0:T(8,128)(2,1)S(1)}, bf16[1024,256]{1,0:T(8,128)(2,1)}, u32[]{:S(2)}) copy-start(bf16[1024,256]{1,0:T(8,128)(2,1)} %counters.1) | copy-start | bytes 1572868
  2.1 1.0 %copy-start.2 = (bf16[256,1024]{1,0:T(8,128)(2,1)S(1)}, bf16[256,1024]{1,0:T(8,128)(2,1)}, u32[]{:S(2)}) copy-start(bf16[256,1024]{1,0:T(8,128)(2,1)} %signatures.1) | copy-start | bytes 1572868
  3.1 1.0 %copy-start.3 = (bf16[1024,256]{1,0:T(8,128)(2,1)S(1)}, bf16[1024,256]{1,0:T(8,128)(2,1)}, u32[]{:S(2)}) copy-start(bf16[1024,256]{1,0:T(8,128)(2,1)} %constant.5.clone.inverse) | copy-start | bytes 1572868
  4.2 1.0 %copy-start.4 = (bf16[512,512]{1,0:T(8,128)(2,1)S(1)}, bf16[512,512]{1,0:T(8,128)(2,1)}, u32[]{:S(2)}) copy-start(bf16[512,512]{1,0:T(8,128)(2,1)} %constant.4.clone.forward) | copy-start | bytes 1572868
  5.2 0.9 %copy-start.5 = (bf16[32,4096]{1,0:T(8,128)(2,1)S(1)}, bf16[32,4096]{1,0:T(8,128)(2,1)}, u32[]{:S(2)}) copy-start(bf16[32,4096]{1,0:T(8,128)(2,1)} %taps.1) | copy-start | bytes 786436
where the time goes:
time: 40.1 us; the launch traced here: 39.8 us
  Pallas kernels  33.6 us (84%)
  local copies, waits for them, and re-layouts  6.15 us (15%)
    pallas_call x1, Pallas kernels, response_call(): pl.pallas_call(functools.partial(response_kernel, plan), out_shape=jax.Sh...  30.9 us
    unnamed x12, local copies, waits for them, and re-layouts  6.15 us
    pallas_call x1, Pallas kernels, output_call(): pl.pallas_call(functools.partial(output_kernel, plan), grid=(plan.blocks,...  2.66 us

commit v1 on v0

--- a/solution.py
+++ b/solution.py
@@ -10,6 +10,7 @@
 from jax.sharding import PartitionSpec as P
 
 MESH = pl.DeviceIdType.MESH
+LARGE_GRANT = 64936 * 1024
 F32 = jnp.float32
 BF16 = jnp.bfloat16
 NT = (((1,), (1,)), ((), ()))
@@ -50,6 +51,9 @@
         self.reach = min((span - 2) // cycles + 1, tm - 1)
         self.ways = min(tm, own // 8)
         self.line = port // 2
+        self.group = min(16, own)
+        self.groups = own // self.group
+        self.pieces = 2
 
 
 def response_kernel(
@@ -58,6 +62,7 @@
     load_sem, part_send, part_recv, merged_send, merged_recv, modal_send, modal_recv, out_send, out_recv,
 ):
     T, N, W, C, R, own = plan.tm, plan.port, plan.width, plan.blocks, plan.reach, plan.own
+    G, M = plan.groups, plan.group
     t, p = lax.axis_index("tm"), lax.axis_index("port")
     loads = [
         pltpu.make_async_copy(src, dst, load_sem.at[i])
@@ -115,9 +120,7 @@
     quad = 4
 
     def taps_step(i, carry):
-        rows = [
-            tap[:, pl.ds(pl.multiple_of((i * quad + j) * W, W), W)] for j in range(quad)
-        ]
+        rows = [tap[:, pl.ds(pl.multiple_of((i * quad + j) * W, W), W)] for j in range(quad)]
         result = transform(jnp.concatenate(rows, axis=0))
         taps_spectra[pl.ds(i * quad, quad)] = result.reshape(quad, own, 2 * W)
         return carry
@@ -157,39 +160,30 @@
 
     high, low = halves(merged[...].reshape(own, plan.tallies))
     both = lax.dot_general(jnp.concatenate([high, low], axis=0), cnt[...], NT, preferred_element_type=F32)
-    xs[0] = (both[:own] + both[own:]).astype(BF16)
-
-    def modal_copy(d):
+    modal = (both[:own] + both[own:]).astype(BF16)
+    xs[0] = modal.reshape(G, M, plan.cycles)
+
+    def modal_copy(d, h):
         return pltpu.make_async_remote_copy(
-            src_ref=xs.at[0],
-            dst_ref=xs.at[d],
-            send_sem=modal_send.at[d],
-            recv_sem=modal_recv.at[d],
+            src_ref=xs.at[0, h],
+            dst_ref=xs.at[d, h],
+            send_sem=modal_send.at[d, h],
+            recv_sem=modal_recv.at[d, h],
             device_id={"tm": t + d, "port": p},
             device_id_type=MESH,
         )
 
-    for d in range(1, R + 1):
-        @pl.when(t + d < T)
-        def _():
-            modal_copy(d).start()
-
-    def spectra_of(d):
-        rows = jnp.concatenate([xs[d, :, i * W : (i + 1) * W] for i in range(C)], axis=0)
-        spectra[(R - d) * C : (R - d + 1) * C] = transform(rows).reshape(C, own, 2 * W)
-
-    spectra_of(0)
-    for d in range(1, R + 1):
-        @pl.when(t >= d)
-        def _():
-            modal_copy(d).wait_recv()
-
-        spectra_of(d)
+    for h in range(G):
+        for d in range(1, R + 1):
+            @pl.when(t + d < T)
+            def _():
+                modal_copy(d, h).start()
 
     sign = 1.0 - 2.0 * (lax.broadcasted_iota(jnp.int32, (8, 128), 1) % 2).astype(F32)
 
-    def product_step(g, carry):
+    def product_step(h, g):
         rows = pl.ds(pl.multiple_of(g * 8, 8), 8)
+        taps_rows = pl.ds(pl.multiple_of(h * M + g * 8, 8), 8)
         for q in range(W // 128):
             re, im = slice(q * 128, q * 128 + 128), slice(W + q * 128, W + q * 128 + 128)
             acc_re, acc_im = [None] * C, [None] * C
@@ -203,80 +197,105 @@
                 for a in range(C):
                     lag = a - j
                     if 0 <= lag < plan.lags:
-                        h_re, h_im = taps_spectra[lag, rows, re], taps_spectra[lag, rows, im]
+                        h_re, h_im = taps_spectra[lag, taps_rows, re], taps_spectra[lag, taps_rows, im]
                         add_re, add_im = h_re * z_re - h_im * z_im, h_re * z_im + h_im * z_re
                         acc_re[a] = add_re if acc_re[a] is None else acc_re[a] + add_re
                         acc_im[a] = add_im if acc_im[a] is None else acc_im[a] + add_im
             for a in range(C):
                 product[a, rows, re] = acc_re[a]
                 product[a, rows, im] = acc_im[a]
-        return carry
-
-    lax.fori_loop(0, own // 8, product_step, 0)
-    loads[5].wait()
-    high, low = halves(product[...].reshape(C * own, 2 * W))
-    result = dot(high, inv[: 2 * W]) + dot(low, inv[: 2 * W]) + dot(high, inv[2 * W :])
-    out[p] = result.astype(BF16).reshape(C, own, W)
 
     place, side = p // 2, lax.rem(p, 2)
-
-    def out_copy(piece, c, way, to):
+    S = plan.pieces
+    wide = plan.cycles // S
+    up, down, partner = 0, 1, 2
+    mate = p + 1 - 2 * side
+
+    def out_copy(piece, i, way, to):
+        h = i // S
+        c = lax.rem(i, S)
+        part = out.at[piece, h, :, pl.ds(pl.multiple_of(c * wide, wide), wide)]
         return pltpu.make_async_remote_copy(
-            src_ref=out.at[piece, c],
-            dst_ref=out.at[piece, c],
-            send_sem=out_send.at[piece, c, way],
-            recv_sem=out_recv.at[piece, c],
+            src_ref=part,
+            dst_ref=part,
+            send_sem=out_send.at[piece, i, way],
+            recv_sem=out_recv.at[piece, i],
             device_id={"tm": t, "port": to},
             device_id_type=MESH,
         )
 
-    up, down, partner = 0, 1, 2
-    mate = p + 1 - 2 * side
-
-    def send_own(c, carry):
-        @pl.when(place + 1 < plan.line)
-        def _():
-            out_copy(p, c, up, p + 2).start()
-
-        @pl.when(place >= 1)
-        def _():
-            out_copy(p, c, down, p - 2).start()
-
-        out_copy(p, c, partner, mate).start()
+    loads[5].wait()
+
+    def group_step(h, carry):
+        for d in range(1, R + 1):
+            @pl.when(t >= d)
+            def _():
+                modal_copy(d, h).wait_recv()
+
+        rows = [
+            xs[d, h, :, i * W : (i + 1) * W] for d in range(R, -1, -1) for i in range(C)
+        ]
+        spectra[...] = transform(jnp.concatenate(rows, axis=0)).reshape((R + 1) * C, M, 2 * W)
+
+        def step(g, inner):
+            product_step(h, g)
+            return inner
+
+        lax.fori_loop(0, M // 8, step, 0)
+        high, low = halves(product[...].reshape(C * M, 2 * W))
+        result = dot(high, inv[: 2 * W]) + dot(low, inv[: 2 * W]) + dot(high, inv[2 * W :])
+        result = result.astype(BF16)
+        for a in range(C):
+            out[p, h, :, a * W : (a + 1) * W] = result[a * M : (a + 1) * M]
+
+        for c in range(S):
+            i = h * S + c
+
+            @pl.when(place + 1 < plan.line)
+            def _():
+                out_copy(p, i, up, p + 2).start()
+
+            @pl.when(place >= 1)
+            def _():
+                out_copy(p, i, down, p - 2).start()
+
+            out_copy(p, i, partner, mate).start()
+
         return carry
 
-    lax.fori_loop(0, C, send_own, 0)
+    lax.fori_loop(0, G, group_step, 0)
+
     for k in range(1, plan.line):
-        def forward_step(c, carry):
+        def forward_step(i, carry):
             @pl.when(place >= k)
             def _():
                 piece = p - 2 * k
-                out_copy(piece, c, up, p).wait_recv()
+                out_copy(piece, i, up, p).wait_recv()
 
                 @pl.when(place + 1 < plan.line)
                 def _():
-                    out_copy(piece, c, up, p + 2).start()
-
-                out_copy(piece, c, partner, mate).start()
+                    out_copy(piece, i, up, p + 2).start()
+
+                out_copy(piece, i, partner, mate).start()
 
             @pl.when(place + k < plan.line)
             def _():
                 piece = p + 2 * k
-                out_copy(piece, c, down, p).wait_recv()
+                out_copy(piece, i, down, p).wait_recv()
 
                 @pl.when(place >= 1)
                 def _():
-                    out_copy(piece, c, down, p - 2).start()
-
-                out_copy(piece, c, partner, mate).start()
+                    out_copy(piece, i, down, p - 2).start()
+
+                out_copy(piece, i, partner, mate).start()
 
             return carry
 
-        lax.fori_loop(0, C, forward_step, 0)
+        lax.fori_loop(0, G * S, forward_step, 0)
 
     def finish(i, carry):
-        c = lax.rem(i, C)
-        z = i // C
+        c = lax.rem(i, G * S)
+        z = i // (G * S)
         out_copy(2 * z + 1 - side, c, partner, mate).wait_recv()
         piece = 2 * z + side
         out_copy(piece, c, partner, mate).wait_send()
@@ -291,7 +310,7 @@
 
         return carry
 
-    lax.fori_loop(0, plan.line * C, finish, 0)
+    lax.fori_loop(0, plan.line * G * S, finish, 0)
     for k in range(1, N):
         part_copy(k).wait_send()
     for k in range(1, plan.ways):
@@ -299,15 +318,17 @@
     for d in range(1, R + 1):
         @pl.when(t + d < T)
         def _():
-            modal_copy(d).wait_send()
+            for h in range(G):
+                modal_copy(d, h).wait_send()
 
 
 def response_call(plan, counters, signatures, eigen, taps, forward, inverse):
     T, N, W, C, R, own = plan.tm, plan.port, plan.width, plan.blocks, plan.reach, plan.own
+    G, M, S = plan.groups, plan.group, plan.pieces
     dma = pltpu.SemaphoreType.DMA
     return pl.pallas_call(
         functools.partial(response_kernel, plan),
-        out_shape=jax.ShapeDtypeStruct((N, C, own, W), BF16),
+        out_shape=jax.ShapeDtypeStruct((N, G, M, plan.cycles), BF16),
         in_specs=[pl.BlockSpec(memory_space=pl.ANY)] * 6,
         out_specs=pl.BlockSpec(memory_space=pltpu.VMEM),
         scratch_shapes=[
@@ -320,15 +341,15 @@
             pltpu.VMEM((N * own, plan.tallies), F32),
             pltpu.VMEM((N, 8, plan.tallies), F32),
             pltpu.VMEM((plan.ways, 8, plan.tallies), F32),
-            pltpu.VMEM((R + 1, own, plan.cycles), BF16),
-            pltpu.VMEM(((R + 1) * C, own, 2 * W), F32),
+            pltpu.VMEM((R + 1, G, M, plan.cycles), BF16),
+            pltpu.VMEM(((R + 1) * C, M, 2 * W), F32),
             pltpu.VMEM((plan.lags, own, 2 * W), F32),
-            pltpu.VMEM((C, own, 2 * W), F32),
+            pltpu.VMEM((C, M, 2 * W), F32),
             dma((6,)), dma((N,)), dma((N,)), dma((plan.ways,)), dma((plan.ways,)),
-            dma((R + 1,)), dma((R + 1,)), dma((N, C, 3)), dma((N, C)),
+            dma((R + 1, G)), dma((R + 1, G)), dma((N, G * S, 3)), dma((N, G * S)),
         ],
         compiler_params=pltpu.CompilerParams(
-            collective_id=0, has_side_effects=True, vmem_limit_bytes=32 * 1024 * 1024
+            collective_id=0, has_side_effects=True, vmem_limit_bytes=LARGE_GRANT
         ),
         name="response",
     )(counters, signatures, eigen, taps, forward, inverse)
@@ -346,11 +367,11 @@
         grid=(plan.blocks,),
         out_shape=jax.ShapeDtypeStruct((plan.cycles, plan.ports), BF16),
         in_specs=[
-            pl.BlockSpec((plan.port, None, plan.own, plan.width), lambda a: (0, a, 0, 0)),
+            pl.BlockSpec((plan.port, plan.groups, plan.group, plan.width), lambda a: (0, 0, 0, a)),
             pl.BlockSpec(eigen.shape, lambda a: (0, 0)),
         ],
         out_specs=pl.BlockSpec((plan.width, plan.ports), lambda a: (a, 0)),
-        compiler_params=pltpu.CompilerParams(vmem_limit_bytes=24 * 1024 * 1024),
+        compiler_params=pltpu.CompilerParams(vmem_limit_bytes=LARGE_GRANT),
         name="output",
     )(response, eigen)
 

time: 40.1 us -> 35.3 us (0.88)
  local copies, waits for them, and re-layouts: 6.15 us -> 0 us
  Pallas kernels: 33.6 us -> 35.1 us
    unnamed x12 -> x0, local copies, waits for them, and re-layouts: 6.15 us -> none
    pallas_call x1, Pallas kernels: 2.66 us -> 4.31 us  [output_call(): pl.pallas_call(functools.partial(output_kernel, plan), grid=(plan.blocks,...]
where the time goes in v1:
time: 35.3 us; the launch traced here: 35.1 us
  Pallas kernels  35.1 us (99%)
    pallas_call x1, Pallas kernels, response_call(): pl.pallas_call(functools.partial(response_kernel, plan), out_shape=jax.Sh...  30.8 us
    pallas_call x1, Pallas kernels, output_call(): pl.pallas_call(functools.partial(output_kernel, plan), grid=(plan.blocks,...  4.31 us

profile of v1, /device:TPU:2, one launch (start us, length us, event | category | flops | bytes accessed | tf_op | source)
XLA Modules:
  0.0 35.1 jit_solution(8884924388073226201)
XLA Ops:
  0.0 30.8 %response.1 = bf16[8,2,16,1024]{3,2,1,0:T(8,128)(2,1)} custom-call(bf16[1024,256]{1,0:T(8,128)(2,1)} %counters.1, bf16[256,1024]{1,0:T(8,128)(2,1)} %signatures.1, bf16[1024,256]{1,0:T(8,128)(2,1)} %eigen.3, bf16[32,4096]{1,0:T(8,128)(2,1)} %taps.1, bf16[512,512]{1,0:T(8,128)(2,1)} %constant.4.clone.forward, bf16[1024,256]{1,0:T(8,128)(2,1)} %constant.5.clone.inverse), custom_call_target="tpu_custom_call" | custom-call | tf_op jit(solution)/shard_map/response/pallas_call | solution.py:329
  30.8 4.3 %output.1 = bf16[1024,1024]{1,0:T(8,128)(2,1)} custom-call(bf16[8,2,16,1024]{3,2,1,0:T(8,128)(2,1)} %response.1, bf16[1024,256]{1,0:T(8,128)(2,1)} %eigen.3), custom_call_target="tpu_custom_call" | custom-call | tf_op jit(solution)/shard_map/output/pallas_call | solution.py:365

commit v2 on v1

--- a/solution.py
+++ b/solution.py
@@ -10,7 +10,7 @@
 from jax.sharding import PartitionSpec as P
 
 MESH = pl.DeviceIdType.MESH
-LARGE_GRANT = 64936 * 1024
+LARGE_GRANT = 60 * 1024 * 1024
 F32 = jnp.float32
 BF16 = jnp.bfloat16
 NT = (((1,), (1,)), ((), ()))
@@ -50,6 +50,7 @@
         self.lags = span // self.width
         self.reach = min((span - 2) // cycles + 1, tm - 1)
         self.ways = min(tm, own // 8)
+        self.rows = own // self.ways
         self.line = port // 2
         self.group = min(16, own)
         self.groups = own // self.group
@@ -100,7 +101,7 @@
     def part_copy(k):
         to = lax.rem(p + k, N)
         return pltpu.make_async_remote_copy(
-            src_ref=partial.at[pl.ds(pl.multiple_of(to * own + share * 8, 8), 8)],
+            src_ref=partial.at[pl.ds(pl.multiple_of(to * own + share * plan.rows, 8), plan.rows)],
             dst_ref=parts.at[k],
             send_sem=part_send.at[k],
             recv_sem=part_recv.at[k],
@@ -131,7 +132,7 @@
         def _():
             xs[d] = jnp.zeros_like(xs[d])
 
-    total = partial[pl.ds(pl.multiple_of(p * own + share * 8, 8), 8)]
+    total = partial[pl.ds(pl.multiple_of(p * own + share * plan.rows, 8), plan.rows)]
     for k in range(1, N):
         part_copy(k).wait_recv()
         total = total + parts[k]
@@ -208,7 +209,7 @@
     place, side = p // 2, lax.rem(p, 2)
     S = plan.pieces
     wide = plan.cycles // S
-    up, down, partner = 0, 1, 2
+    partner = 0
     mate = p + 1 - 2 * side
 
     def out_copy(piece, i, way, to):
@@ -251,13 +252,14 @@
         for c in range(S):
             i = h * S + c
 
-            @pl.when(place + 1 < plan.line)
-            def _():
-                out_copy(p, i, up, p + 2).start()
-
-            @pl.when(place >= 1)
-            def _():
-                out_copy(p, i, down, p - 2).start()
+            for k in range(1, plan.line):
+                @pl.when(place + k < plan.line)
+                def _():
+                    out_copy(p, i, k, p + 2 * k).start()
+
+                @pl.when(place >= k)
+                def _():
+                    out_copy(p, i, plan.line + k, p - 2 * k).start()
 
             out_copy(p, i, partner, mate).start()
 
@@ -267,27 +269,11 @@
 
     for k in range(1, plan.line):
         def forward_step(i, carry):
-            @pl.when(place >= k)
-            def _():
-                piece = p - 2 * k
-                out_copy(piece, i, up, p).wait_recv()
-
-                @pl.when(place + 1 < plan.line)
+            for there, piece in ((place >= k, p - 2 * k), (place + k < plan.line, p + 2 * k)):
+                @pl.when(there)
                 def _():
-                    out_copy(piece, i, up, p + 2).start()
-
-                out_copy(piece, i, partner, mate).start()
-
-            @pl.when(place + k < plan.line)
-            def _():
-                piece = p + 2 * k
-                out_copy(piece, i, down, p).wait_recv()
-
-                @pl.when(place >= 1)
-                def _():
-                    out_copy(piece, i, down, p - 2).start()
-
-                out_copy(piece, i, partner, mate).start()
+                    out_copy(piece, i, partner, mate).wait_recv()
+                    out_copy(piece, i, partner, mate).start()
 
             return carry
 
@@ -300,17 +286,22 @@
         piece = 2 * z + side
         out_copy(piece, c, partner, mate).wait_send()
 
-        @pl.when((z <= place) & (place + 1 < plan.line))
-        def _():
-            out_copy(piece, c, up, p).wait_send()
-
-        @pl.when((z >= place) & (place >= 1))
-        def _():
-            out_copy(piece, c, down, p).wait_send()
-
         return carry
 
     lax.fori_loop(0, plan.line * G * S, finish, 0)
+    for k in range(1, plan.line):
+        def sent(i, carry):
+            @pl.when(place + k < plan.line)
+            def _():
+                out_copy(p, i, k, p + 2 * k).wait_send()
+
+            @pl.when(place >= k)
+            def _():
+                out_copy(p, i, plan.line + k, p - 2 * k).wait_send()
+
+            return carry
+
+        lax.fori_loop(0, G * S, sent, 0)
     for k in range(1, N):
         part_copy(k).wait_send()
     for k in range(1, plan.ways):
@@ -339,14 +330,14 @@
             pltpu.VMEM(forward.shape, BF16),
             pltpu.VMEM(inverse.shape, BF16),
             pltpu.VMEM((N * own, plan.tallies), F32),
-            pltpu.VMEM((N, 8, plan.tallies), F32),
-            pltpu.VMEM((plan.ways, 8, plan.tallies), F32),
+            pltpu.VMEM((N, plan.rows, plan.tallies), F32),
+            pltpu.VMEM((plan.ways, plan.rows, plan.tallies), F32),
             pltpu.VMEM((R + 1, G, M, plan.cycles), BF16),
             pltpu.VMEM(((R + 1) * C, M, 2 * W), F32),
             pltpu.VMEM((plan.lags, own, 2 * W), F32),
             pltpu.VMEM((C, M, 2 * W), F32),
             dma((6,)), dma((N,)), dma((N,)), dma((plan.ways,)), dma((plan.ways,)),
-            dma((R + 1, G)), dma((R + 1, G)), dma((N, G * S, 3)), dma((N, G * S)),
+            dma((R + 1, G)), dma((R + 1, G)), dma((N, G * S, 2 * plan.line)), dma((N, G * S)),
         ],
         compiler_params=pltpu.CompilerParams(
             collective_id=0, has_side_effects=True, vmem_limit_bytes=LARGE_GRANT
@@ -371,7 +362,7 @@
             pl.BlockSpec(eigen.shape, lambda a: (0, 0)),
         ],
         out_specs=pl.BlockSpec((plan.width, plan.ports), lambda a: (a, 0)),
-        compiler_params=pltpu.CompilerParams(vmem_limit_bytes=LARGE_GRANT),
+        compiler_params=pltpu.CompilerParams(vmem_limit_bytes=24 * 1024 * 1024),
         name="output",
     )(response, eigen)
 

time: 35.3 us -> 35.2 us (level)
  Pallas kernels: 35.1 us -> 34 us
  local copies, waits for them, and re-layouts: 0 us -> 1.04 us
    pallas_call x1, Pallas kernels: 4.31 us -> 2.68 us  [output_call(): pl.pallas_call(functools.partial(output_kernel, plan), grid=(plan.blocks,...]
    unnamed x0 -> x4, local copies, waits for them, and re-layouts: none -> 1.04 us
    pallas_call x1, Pallas kernels: 30.8 us -> 31.3 us  [response_call(): pl.pallas_call(functools.partial(response_kernel, plan), out_shape=jax.Sh...]
where the time goes in v2:
time: 35.2 us; the launch traced here: 35.1 us
  Pallas kernels  34 us (97%)
  local copies, waits for them, and re-layouts  1.04 us (3%)
    pallas_call x1, Pallas kernels, response_call(): pl.pallas_call(functools.partial(response_kernel, plan), out_shape=jax.Sh...  31.3 us
    pallas_call x1, Pallas kernels, output_call(): pl.pallas_call(functools.partial(output_kernel, plan), grid=(plan.blocks,...  2.68 us
    unnamed x4, local copies, waits for them, and re-layouts  1.04 us

profile of v2, /device:TPU:2, one launch (start us, length us, event | category | flops | bytes accessed | tf_op | source)
XLA Modules:
  0.0 35.1 jit_solution(8110210400165591661)
XLA Ops:
  0.0 0.0 copy-start
  0.0 31.3 %response.1 = bf16[8,2,16,1024]{3,2,1,0:T(8,128)(2,1)} custom-call(bf16[1024,256]{1,0:T(8,128)(2,1)} %counters.1, bf16[256,1024]{1,0:T(8,128)(2,1)} %signatures.1, bf16[1024,256]{1,0:T(8,128)(2,1)} %eigen.3, bf16[32,4096]{1,0:T(8,128)(2,1)} %taps.1, bf16[512,512]{1,0:T(8,128)(2,1)} %constant.4.clone.forward, bf16[1024,256]{1,0:T(8,128)(2,1)} %constant.5.clone.inverse), custom_call_target="tpu_custom_call" | custom-call | tf_op jit(solution)/shard_map/response/pallas_call | solution.py:320
  31.3 0.0 copy-done
  31.4 0.0 copy-start.1
  31.4 1.0 %copy-done.1 = bf16[8,2,16,1024]{3,2,1,0:T(8,128)(2,1)S(1)} copy-done((bf16[8,2,16,1024]{3,2,1,0:T(8,128)(2,1)S(1)}, bf16[8,2,16,1024]{3,2,1,0:T(8,128)(2,1)}, u32[]{:S(2)}) %copy-start.1) | copy-done | bytes 524312
  32.4 2.7 %output.1 = bf16[1024,1024]{1,0:T(8,128)(2,1)} custom-call(bf16[8,2,16,1024]{3,2,1,0:T(8,128)(2,1)S(1)} %copy-done.1, bf16[1024,256]{1,0:T(8,128)(2,1)S(1)} %copy-done), custom_call_target="tpu_custom_call" | custom-call | tf_op jit(solution)/shard_map/output/pallas_call | solution.py:356
Async XLA Ops:
  0.0 31.3 %copy-start = (bf16[1024,256]{1,0:T(8,128)(2,1)S(1)}, bf16[1024,256]{1,0:T(8,128)(2,1)}, u32[]{:S(2)}) copy-start(bf16[1024,256]{1,0:T(8,128)(2,1)} %eigen.3) | copy-start | bytes 1572868
  31.4 1.0 %copy-start.1 = (bf16[8,2,16,1024]{3,2,1,0:T(8,128)(2,1)S(1)}, bf16[8,2,16,1024]{3,2,1,0:T(8,128)(2,1)}, u32[]{:S(2)}) copy-start(bf16[8,2,16,1024]{3,2,1,0:T(8,128)(2,1)} %response.1) | copy-start | bytes 1572868

commit v3 on v1

--- a/solution.py
+++ b/solution.py
@@ -10,7 +10,7 @@
 from jax.sharding import PartitionSpec as P
 
 MESH = pl.DeviceIdType.MESH
-LARGE_GRANT = 64936 * 1024
+LARGE_GRANT = 60 * 1024 * 1024
 F32 = jnp.float32
 BF16 = jnp.bfloat16
 NT = (((1,), (1,)), ((), ()))
@@ -50,16 +50,17 @@
         self.lags = span // self.width
         self.reach = min((span - 2) // cycles + 1, tm - 1)
         self.ways = min(tm, own // 8)
+        self.rows = own // self.ways
         self.line = port // 2
         self.group = min(16, own)
         self.groups = own // self.group
         self.pieces = 2
 
 
-def response_kernel(
-    plan, counters, signatures, eigen, taps, forward, inverse, out,
-    cnt, sig, eig, tap, fwd, inv, partial, parts, merged, xs, spectra, taps_spectra, product,
-    load_sem, part_send, part_recv, merged_send, merged_recv, modal_send, modal_recv, out_send, out_recv,
+def sag_kernel(
+    plan, counters, signatures, eigen, taps, forward, inverse, sag,
+    cnt, sig, eig, tap, fwd, inv, partial, parts, merged, xs, spectra, taps_spectra, product, out, turned, total, rounded,
+    load_sem, part_send, part_recv, merged_send, merged_recv, modal_send, modal_recv, out_send, out_recv, sag_sem,
 ):
     T, N, W, C, R, own = plan.tm, plan.port, plan.width, plan.blocks, plan.reach, plan.own
     G, M = plan.groups, plan.group
@@ -100,7 +101,7 @@
     def part_copy(k):
         to = lax.rem(p + k, N)
         return pltpu.make_async_remote_copy(
-            src_ref=partial.at[pl.ds(pl.multiple_of(to * own + share * 8, 8), 8)],
+            src_ref=partial.at[pl.ds(pl.multiple_of(to * own + share * plan.rows, 8), plan.rows)],
             dst_ref=parts.at[k],
             send_sem=part_send.at[k],
             recv_sem=part_recv.at[k],
@@ -126,16 +127,22 @@
         return carry
 
     lax.fori_loop(0, plan.lags // quad, taps_step, 0)
+    tile = min(256, plan.ports)
+    for i in range(plan.ports // tile):
+        block = eig[i * tile : (i + 1) * tile].T
+        for piece in range(N):
+            z, b = divmod(piece, 2)
+            turned[b, z * own : (z + 1) * own, i * tile : (i + 1) * tile] = block[piece * own : (piece + 1) * own]
     for d in range(1, R + 1):
         @pl.when(t < d)
         def _():
             xs[d] = jnp.zeros_like(xs[d])
 
-    total = partial[pl.ds(pl.multiple_of(p * own + share * 8, 8), 8)]
+    octet = partial[pl.ds(pl.multiple_of(p * own + share * plan.rows, 8), plan.rows)]
     for k in range(1, N):
         part_copy(k).wait_recv()
-        total = total + parts[k]
-    merged[share] = total
+        octet = octet + parts[k]
+    merged[share] = octet
 
     def merged_copy(k):
         mate = t - share + lax.rem(share + k, plan.ways)
@@ -208,13 +215,15 @@
     place, side = p // 2, lax.rem(p, 2)
     S = plan.pieces
     wide = plan.cycles // S
-    up, down, partner = 0, 1, 2
+    up, down, partner, across = 0, 1, 2, 3
     mate = p + 1 - 2 * side
+    pair = place + 1 - 2 * lax.rem(place, 2)
+    paired = 2 * pair + side
 
     def out_copy(piece, i, way, to):
         h = i // S
         c = lax.rem(i, S)
-        part = out.at[piece, h, :, pl.ds(pl.multiple_of(c * wide, wide), wide)]
+        part = out.at[lax.rem(piece, 2), piece // 2, h, :, pl.ds(pl.multiple_of(c * wide, wide), wide)]
         return pltpu.make_async_remote_copy(
             src_ref=part,
             dst_ref=part,
@@ -246,7 +255,7 @@
         result = dot(high, inv[: 2 * W]) + dot(low, inv[: 2 * W]) + dot(high, inv[2 * W :])
         result = result.astype(BF16)
         for a in range(C):
-            out[p, h, :, a * W : (a + 1) * W] = result[a * M : (a + 1) * M]
+            out[side, place, h, :, a * W : (a + 1) * W] = result[a * M : (a + 1) * M]
 
         for c in range(S):
             i = h * S + c
@@ -270,47 +279,103 @@
             @pl.when(place >= k)
             def _():
                 piece = p - 2 * k
-                out_copy(piece, i, up, p).wait_recv()
+                out_copy(piece, i, up, mate).wait_recv()
 
                 @pl.when(place + 1 < plan.line)
                 def _():
                     out_copy(piece, i, up, p + 2).start()
 
-                out_copy(piece, i, partner, mate).start()
+                @pl.when((piece != paired) | (lax.rem(i, 2) == 0))
+                def _():
+                    out_copy(piece, i, partner, mate).start()
 
             @pl.when(place + k < plan.line)
             def _():
                 piece = p + 2 * k
-                out_copy(piece, i, down, p).wait_recv()
+                out_copy(piece, i, down, mate).wait_recv()
 
                 @pl.when(place >= 1)
                 def _():
                     out_copy(piece, i, down, p - 2).start()
 
-                out_copy(piece, i, partner, mate).start()
+                @pl.when((piece != paired) | (lax.rem(i, 2) == 0))
+                def _():
+                    out_copy(piece, i, partner, mate).start()
+
+            if k == 1:
+                @pl.when(lax.rem(i, 2) == 1)
+                def _():
+                    out_copy(mate, i, across, mate).wait_recv()
+                    out_copy(mate, i, across, paired).start()
 
             return carry
 
         lax.fori_loop(0, G * S, forward_step, 0)
 
-    def finish(i, carry):
-        c = lax.rem(i, G * S)
-        z = i // (G * S)
-        out_copy(2 * z + 1 - side, c, partner, mate).wait_recv()
+    modes = plan.line * own
+
+    def side_part(b, a):
+        columns = pl.ds(pl.multiple_of(a * W, W), W)
+        block = out[b, :, :, :, columns].reshape(modes, W).T
+        return dot(block, turned[b])
+
+    def first_side(a, carry):
+        total[pl.ds(pl.multiple_of(a * W, W), W)] = side_part(side, a)
+        return carry
+
+    lax.fori_loop(0, C, first_side, 0)
+
+    def sag_copy(a):
+        rows = pl.ds(pl.multiple_of(a * W, W), W)
+        return pltpu.make_async_copy(rounded.at[rows], sag.at[rows], sag_sem.at[a])
+
+    def second_side(c, carry):
+        for z in range(plan.line):
+            for h in range(G):
+                i = h * S + c
+
+                @pl.when((z != place) | (c == 0))
+                def _():
+                    out_copy(2 * z + 1 - side, i, partner, mate).wait_recv()
+
+        def step(j, inner):
+            a = c * (C // S) + j
+            rows = pl.ds(pl.multiple_of(a * W, W), W)
+            rounded[rows] = (total[rows] + side_part(1 - side, a)).astype(BF16)
+            sag_copy(a).start()
+            return inner
+
+        lax.fori_loop(0, C // S, step, 0)
+        return carry
+
+    lax.fori_loop(0, S, second_side, 0)
+
+    def finish(n, carry):
+        i = lax.rem(n, G * S)
+        z = n // (G * S)
         piece = 2 * z + side
-        out_copy(piece, c, partner, mate).wait_send()
+
+        @pl.when((z != pair) | (lax.rem(i, 2) == 0))
+        def _():
+            out_copy(piece, i, partner, mate).wait_send()
+
+        @pl.when((z == place) & (lax.rem(i, 2) == 1))
+        def _():
+            out_copy(mate, i, across, mate).wait_send()
 
         @pl.when((z <= place) & (place + 1 < plan.line))
         def _():
-            out_copy(piece, c, up, p).wait_send()
+            out_copy(piece, i, up, mate).wait_send()
 
         @pl.when((z >= place) & (place >= 1))
         def _():
-            out_copy(piece, c, down, p).wait_send()
+            out_copy(piece, i, down, mate).wait_send()
 
         return carry
 
     lax.fori_loop(0, plan.line * G * S, finish, 0)
+    for a in range(C):
+        sag_copy(a).wait()
     for k in range(1, N):
         part_copy(k).wait_send()
     for k in range(1, plan.ways):
@@ -322,15 +387,15 @@
                 modal_copy(d, h).wait_send()
 
 
-def response_call(plan, counters, signatures, eigen, taps, forward, inverse):
+def sag_call(plan, counters, signatures, eigen, taps, forward, inverse):
     T, N, W, C, R, own = plan.tm, plan.port, plan.width, plan.blocks, plan.reach, plan.own
     G, M, S = plan.groups, plan.group, plan.pieces
     dma = pltpu.SemaphoreType.DMA
     return pl.pallas_call(
-        functools.partial(response_kernel, plan),
-        out_shape=jax.ShapeDtypeStruct((N, G, M, plan.cycles), BF16),
+        functools.partial(sag_kernel, plan),
+        out_shape=jax.ShapeDtypeStruct((plan.cycles, plan.ports), BF16),
         in_specs=[pl.BlockSpec(memory_space=pl.ANY)] * 6,
-        out_specs=pl.BlockSpec(memory_space=pltpu.VMEM),
+        out_specs=pl.BlockSpec(memory_space=pl.ANY),
         scratch_shapes=[
             pltpu.VMEM(counters.shape, BF16),
             pltpu.VMEM(signatures.shape, BF16),
@@ -339,41 +404,24 @@
             pltpu.VMEM(forward.shape, BF16),
             pltpu.VMEM(inverse.shape, BF16),
             pltpu.VMEM((N * own, plan.tallies), F32),
-            pltpu.VMEM((N, 8, plan.tallies), F32),
-            pltpu.VMEM((plan.ways, 8, plan.tallies), F32),
+            pltpu.VMEM((N, plan.rows, plan.tallies), F32),
+            pltpu.VMEM((plan.ways, plan.rows, plan.tallies), F32),
             pltpu.VMEM((R + 1, G, M, plan.cycles), BF16),
             pltpu.VMEM(((R + 1) * C, M, 2 * W), F32),
             pltpu.VMEM((plan.lags, own, 2 * W), F32),
             pltpu.VMEM((C, M, 2 * W), F32),
+            pltpu.VMEM((2, plan.line, G, M, plan.cycles), BF16),
+            pltpu.VMEM((2, plan.line * own, plan.ports), BF16),
+            pltpu.VMEM((plan.cycles, plan.ports), F32),
+            pltpu.VMEM((plan.cycles, plan.ports), BF16),
             dma((6,)), dma((N,)), dma((N,)), dma((plan.ways,)), dma((plan.ways,)),
-            dma((R + 1, G)), dma((R + 1, G)), dma((N, G * S, 3)), dma((N, G * S)),
+            dma((R + 1, G)), dma((R + 1, G)), dma((N, G * S, 4)), dma((N, G * S)), dma((C,)),
         ],
         compiler_params=pltpu.CompilerParams(
             collective_id=0, has_side_effects=True, vmem_limit_bytes=LARGE_GRANT
         ),
-        name="response",
+        name="sag",
     )(counters, signatures, eigen, taps, forward, inverse)
-
-
-def output_kernel(plan, response, eigen, out):
-    block = response[...].reshape(plan.port * plan.own, plan.width)
-    turned = block.T
-    out[...] = lax.dot_general(turned, eigen[...], NT, preferred_element_type=F32).astype(BF16)
-
-
-def output_call(plan, response, eigen):
-    return pl.pallas_call(
-        functools.partial(output_kernel, plan),
-        grid=(plan.blocks,),
-        out_shape=jax.ShapeDtypeStruct((plan.cycles, plan.ports), BF16),
-        in_specs=[
-            pl.BlockSpec((plan.port, plan.groups, plan.group, plan.width), lambda a: (0, 0, 0, a)),
-            pl.BlockSpec(eigen.shape, lambda a: (0, 0)),
-        ],
-        out_specs=pl.BlockSpec((plan.width, plan.ports), lambda a: (a, 0)),
-        compiler_params=pltpu.CompilerParams(vmem_limit_bytes=LARGE_GRANT),
-        name="output",
-    )(response, eigen)
 
 
 def solution(mesh):
@@ -383,10 +431,9 @@
             counters.shape[1], taps.shape[0], taps.shape[1],
         )
         forward, inverse = odd_dft(plan.width)
-        response = response_call(
+        return sag_call(
             plan, counters, signatures, eigen, taps, jnp.asarray(forward), jnp.asarray(inverse)
         )
-        return output_call(plan, response, eigen)
 
     in_specs = (P("tm", None), P(None, "port"), P("port", None), P("port", None))
     return jax.shard_map(

time: 35.3 us -> 35.5 us (level)
  local copies, waits for them, and re-layouts: 0 us -> 3.08 us
  Pallas kernels: 35.1 us -> 32.3 us
    unnamed x0 -> x1, local copies, waits for them, and re-layouts: none -> 3.08 us
    pallas_call x2 -> x1, Pallas kernels: 35.1 us -> 32.3 us  [sag_call(): pl.pallas_call(functools.partial(sag_kernel, plan), out_shape=jax.ShapeDt...]
where the time goes in v3:
time: 35.5 us; the launch traced here: 35.4 us
  Pallas kernels  32.3 us (91%)
  local copies, waits for them, and re-layouts  3.08 us (9%)
    pallas_call x1, Pallas kernels, sag_call(): pl.pallas_call(functools.partial(sag_kernel, plan), out_shape=jax.ShapeDt...  32.3 us
    unnamed x1, local copies, waits for them, and re-layouts  3.08 us

profile of v3, /device:TPU:2, one launch (start us, length us, event | category | flops | bytes accessed | tf_op | source)
XLA Modules:
  0.0 35.4 jit_solution(9214596117894108440)
XLA Ops:
  0.0 32.3 %sag.1 = bf16[1024,1024]{1,0:T(8,128)(2,1)} custom-call(bf16[1024,256]{1,0:T(8,128)(2,1)} %counters.1, bf16[256,1024]{1,0:T(8,128)(2,1)} %signatures.1, bf16[1024,256]{1,0:T(8,128)(2,1)} %eigen.1, bf16[32,4096]{1,0:T(8,128)(2,1)} %taps.1, bf16[512,512]{1,0:T(8,128)(2,1)} %constant.4.clone.forward, bf16[1024,256]{1,0:T(8,128)(2,1)} %constant.5.clone.inverse), custom_call_target="tpu_custom_call" | custom-call | tf_op jit(solution)/shard_map/sag/pallas_call | solution.py:394
  32.3 3.1 %copy.8 = bf16[1024,1024]{1,0:T(8,128)(2,1)} copy(bf16[1024,1024]{1,0:T(8,128)(2,1)} %sag.1) | data formatting | bytes 4194304

commit v4 on v3

--- a/solution.py
+++ b/solution.py
@@ -55,6 +55,7 @@
         self.group = min(16, own)
         self.groups = own // self.group
         self.pieces = 2
+        self.strips = 8
 
 
 def sag_kernel(
@@ -424,6 +425,32 @@
     )(counters, signatures, eigen, taps, forward, inverse)
 
 
+def placed_kernel(plan, source, target, sem):
+    rows = plan.cycles // plan.strips
+    copies = [
+        pltpu.make_async_copy(
+            source.at[pl.ds(i * rows, rows)], target.at[pl.ds(i * rows, rows)], sem.at[i]
+        )
+        for i in range(plan.strips)
+    ]
+    for copy in copies:
+        copy.start()
+    for copy in copies:
+        copy.wait()
+
+
+def placed(plan, sag):
+    return pl.pallas_call(
+        functools.partial(placed_kernel, plan),
+        out_shape=jax.ShapeDtypeStruct(sag.shape, sag.dtype),
+        in_specs=[pl.BlockSpec(memory_space=pl.ANY)],
+        out_specs=pl.BlockSpec(memory_space=pl.ANY),
+        scratch_shapes=[pltpu.SemaphoreType.DMA((plan.strips,))],
+        compiler_params=pltpu.CompilerParams(vmem_limit_bytes=LARGE_GRANT),
+        name="placed",
+    )(sag)
+
+
 def solution(mesh):
     def per_device(counters, signatures, eigen, taps):
         plan = Plan(
@@ -431,9 +458,10 @@
             counters.shape[1], taps.shape[0], taps.shape[1],
         )
         forward, inverse = odd_dft(plan.width)
-        return sag_call(
+        sag = sag_call(
             plan, counters, signatures, eigen, taps, jnp.asarray(forward), jnp.asarray(inverse)
         )
+        return placed(plan, sag)
 
     in_specs = (P("tm", None), P(None, "port"), P("port", None), P("port", None))
     return jax.shard_map(

time: 35.5 us -> 97.1 us (2.74)
  Pallas kernels: 32.3 us -> 97 us
  local copies, waits for them, and re-layouts: 3.08 us -> 0 us
    pallas_call x0 -> x1, Pallas kernels: none -> 64.7 us  [placed(): pl.pallas_call(functools.partial(placed_kernel, plan), out_shape=jax.Shap...]
    unnamed x1 -> x0, local copies, waits for them, and re-layouts: 3.08 us -> none
where the time goes in v4:
time: 97.1 us; the launch traced here: 97 us
  Pallas kernels  97 us (100%)
    pallas_call x1, Pallas kernels, placed(): pl.pallas_call(functools.partial(placed_kernel, plan), out_shape=jax.Shap...  64.7 us
    pallas_call x1, Pallas kernels, sag_call(): pl.pallas_call(functools.partial(sag_kernel, plan), out_shape=jax.ShapeDt...  32.3 us

profile of v4, /device:TPU:2, one launch (start us, length us, event | category | flops | bytes accessed | tf_op | source)
XLA Modules:
  0.0 97.0 jit_solution(12107464846911132487)
XLA Ops:
  0.0 32.3 %sag.1.source = bf16[1024,1024]{1,0:T(8,128)(2,1)} custom-call(bf16[1024,256]{1,0:T(8,128)(2,1)} %counters.1, bf16[256,1024]{1,0:T(8,128)(2,1)} %signatures.1, bf16[1024,256]{1,0:T(8,128)(2,1)} %eigen.1, bf16[32,4096]{1,0:T(8,128)(2,1)} %taps.1, bf16[512,512]{1,0:T(8,128)(2,1)} %constant.4.clone.forward, bf16[1024,256]{1,0:T(8,128)(2,1)} %constant.5.clone.inverse), custom_call_target="tpu_custom_call" | custom-call | tf_op jit(solution)/shard_map/sag/pallas_call | solution.py:395
  32.3 64.7 %placed.1 = bf16[1024,1024]{1,0:T(8,128)(2,1)} custom-call(bf16[1024,1024]{1,0:T(8,128)(2,1)} %sag.1.source), custom_call_target="tpu_custom_call" | custom-call | tf_op jit(solution)/shard_map/placed/pallas_call | solution.py:443

commit v5 on v4

--- a/solution.py
+++ b/solution.py
@@ -425,18 +425,23 @@
     )(counters, signatures, eigen, taps, forward, inverse)
 
 
-def placed_kernel(plan, source, target, sem):
-    rows = plan.cycles // plan.strips
-    copies = [
-        pltpu.make_async_copy(
-            source.at[pl.ds(i * rows, rows)], target.at[pl.ds(i * rows, rows)], sem.at[i]
-        )
-        for i in range(plan.strips)
+def placed_kernel(plan, source, target, held, load_sem, store_sem):
+    strips = [pl.ds(i * (plan.cycles // plan.strips), plan.cycles // plan.strips) for i in range(plan.strips)]
+    loads = [
+        pltpu.make_async_copy(source.at[strip], held.at[strip], load_sem.at[i])
+        for i, strip in enumerate(strips)
     ]
-    for copy in copies:
-        copy.start()
-    for copy in copies:
-        copy.wait()
+    stores = [
+        pltpu.make_async_copy(held.at[strip], target.at[strip], store_sem.at[i])
+        for i, strip in enumerate(strips)
+    ]
+    for load in loads:
+        load.start()
+    for load, store in zip(loads, stores):
+        load.wait()
+        store.start()
+    for store in stores:
+        store.wait()
 
 
 def placed(plan, sag):
@@ -445,7 +450,11 @@
         out_shape=jax.ShapeDtypeStruct(sag.shape, sag.dtype),
         in_specs=[pl.BlockSpec(memory_space=pl.ANY)],
         out_specs=pl.BlockSpec(memory_space=pl.ANY),
-        scratch_shapes=[pltpu.SemaphoreType.DMA((plan.strips,))],
+        scratch_shapes=[
+            pltpu.VMEM(sag.shape, sag.dtype),
+            pltpu.SemaphoreType.DMA((plan.strips,)),
+            pltpu.SemaphoreType.DMA((plan.strips,)),
+        ],
         compiler_params=pltpu.CompilerParams(vmem_limit_bytes=LARGE_GRANT),
         name="placed",
     )(sag)

time: 97.1 us -> 34.8 us (0.36)
  Pallas kernels: 97 us -> 34.7 us
    pallas_call x1, Pallas kernels: 64.7 us -> 2.39 us  [placed(): pl.pallas_call(functools.partial(placed_kernel, plan), out_shape=jax.Shap...]
where the time goes in v5:
time: 34.8 us; the launch traced here: 34.7 us
  Pallas kernels  34.7 us (100%)
    pallas_call x1, Pallas kernels, sag_call(): pl.pallas_call(functools.partial(sag_kernel, plan), out_shape=jax.ShapeDt...  32.3 us
    pallas_call x1, Pallas kernels, placed(): pl.pallas_call(functools.partial(placed_kernel, plan), out_shape=jax.Shap...  2.39 us

profile of v5, /device:TPU:2, one launch (start us, length us, event | category | flops | bytes accessed | tf_op | source)
XLA Modules:
  0.0 34.7 jit_solution(13446340815952948939)
XLA Ops:
  0.0 32.3 %sag.1.source = bf16[1024,1024]{1,0:T(8,128)(2,1)} custom-call(bf16[1024,256]{1,0:T(8,128)(2,1)} %counters.1, bf16[256,1024]{1,0:T(8,128)(2,1)} %signatures.1, bf16[1024,256]{1,0:T(8,128)(2,1)} %eigen.1, bf16[32,4096]{1,0:T(8,128)(2,1)} %taps.1, bf16[512,512]{1,0:T(8,128)(2,1)} %constant.4.clone.forward, bf16[1024,256]{1,0:T(8,128)(2,1)} %constant.5.clone.inverse), custom_call_target="tpu_custom_call" | custom-call | tf_op jit(solution)/shard_map/sag/pallas_call | solution.py:395
  32.3 2.4 %placed.1 = bf16[1024,1024]{1,0:T(8,128)(2,1)} custom-call(bf16[1024,1024]{1,0:T(8,128)(2,1)} %sag.1.source), custom_call_target="tpu_custom_call" | custom-call | tf_op jit(solution)/shard_map/placed/pallas_call | solution.py:448

commit v6 on v3

--- a/solution.py
+++ b/solution.py
@@ -57,10 +57,10 @@
         self.pieces = 2
 
 
-def sag_kernel(
-    plan, counters, signatures, eigen, taps, forward, inverse, sag,
-    cnt, sig, eig, tap, fwd, inv, partial, parts, merged, xs, spectra, taps_spectra, product, out, turned, total, rounded,
-    load_sem, part_send, part_recv, merged_send, merged_recv, modal_send, modal_recv, out_send, out_recv, sag_sem,
+def response_kernel(
+    plan, counters, signatures, eigen, taps, forward, inverse, out, turned_out,
+    cnt, sig, eig, tap, fwd, inv, partial, parts, merged, xs, spectra, taps_spectra, product, turned,
+    load_sem, part_send, part_recv, merged_send, merged_recv, modal_send, modal_recv, out_send, out_recv, turned_sem,
 ):
     T, N, W, C, R, own = plan.tm, plan.port, plan.width, plan.blocks, plan.reach, plan.own
     G, M = plan.groups, plan.group
@@ -133,6 +133,8 @@
         for piece in range(N):
             z, b = divmod(piece, 2)
             turned[b, z * own : (z + 1) * own, i * tile : (i + 1) * tile] = block[piece * own : (piece + 1) * own]
+    turned_copy = pltpu.make_async_copy(turned, turned_out, turned_sem)
+    turned_copy.start()
     for d in range(1, R + 1):
         @pl.when(t < d)
         def _():
@@ -312,43 +314,17 @@
 
         lax.fori_loop(0, G * S, forward_step, 0)
 
-    modes = plan.line * own
-
-    def side_part(b, a):
-        columns = pl.ds(pl.multiple_of(a * W, W), W)
-        block = out[b, :, :, :, columns].reshape(modes, W).T
-        return dot(block, turned[b])
-
-    def first_side(a, carry):
-        total[pl.ds(pl.multiple_of(a * W, W), W)] = side_part(side, a)
+    def arrived(n, carry):
+        i = lax.rem(n, G * S)
+        z = n // (G * S)
+
+        @pl.when((z != place) | (lax.rem(i, 2) == 0))
+        def _():
+            out_copy(2 * z + 1 - side, i, partner, mate).wait_recv()
+
         return carry
 
-    lax.fori_loop(0, C, first_side, 0)
-
-    def sag_copy(a):
-        rows = pl.ds(pl.multiple_of(a * W, W), W)
-        return pltpu.make_async_copy(rounded.at[rows], sag.at[rows], sag_sem.at[a])
-
-    def second_side(c, carry):
-        for z in range(plan.line):
-            for h in range(G):
-                i = h * S + c
-
-                @pl.when((z != place) | (c == 0))
-                def _():
-                    out_copy(2 * z + 1 - side, i, partner, mate).wait_recv()
-
-        def step(j, inner):
-            a = c * (C // S) + j
-            rows = pl.ds(pl.multiple_of(a * W, W), W)
-            rounded[rows] = (total[rows] + side_part(1 - side, a)).astype(BF16)
-            sag_copy(a).start()
-            return inner
-
-        lax.fori_loop(0, C // S, step, 0)
-        return carry
-
-    lax.fori_loop(0, S, second_side, 0)
+    lax.fori_loop(0, plan.line * G * S, arrived, 0)
 
     def finish(n, carry):
         i = lax.rem(n, G * S)
@@ -374,8 +350,7 @@
         return carry
 
     lax.fori_loop(0, plan.line * G * S, finish, 0)
-    for a in range(C):
-        sag_copy(a).wait()
+    turned_copy.wait()
     for k in range(1, N):
         part_copy(k).wait_send()
     for k in range(1, plan.ways):
@@ -387,15 +362,18 @@
                 modal_copy(d, h).wait_send()
 
 
-def sag_call(plan, counters, signatures, eigen, taps, forward, inverse):
+def response_call(plan, counters, signatures, eigen, taps, forward, inverse):
     T, N, W, C, R, own = plan.tm, plan.port, plan.width, plan.blocks, plan.reach, plan.own
     G, M, S = plan.groups, plan.group, plan.pieces
     dma = pltpu.SemaphoreType.DMA
     return pl.pallas_call(
-        functools.partial(sag_kernel, plan),
-        out_shape=jax.ShapeDtypeStruct((plan.cycles, plan.ports), BF16),
+        functools.partial(response_kernel, plan),
+        out_shape=(
+            jax.ShapeDtypeStruct((2, plan.line, G, M, plan.cycles), BF16),
+            jax.ShapeDtypeStruct((2, plan.line * own, plan.ports), BF16),
+        ),
         in_specs=[pl.BlockSpec(memory_space=pl.ANY)] * 6,
-        out_specs=pl.BlockSpec(memory_space=pl.ANY),
+        out_specs=(pl.BlockSpec(memory_space=pltpu.VMEM), pl.BlockSpec(memory_space=pl.ANY)),
         scratch_shapes=[
             pltpu.VMEM(counters.shape, BF16),
             pltpu.VMEM(signatures.shape, BF16),
@@ -410,18 +388,61 @@
             pltpu.VMEM(((R + 1) * C, M, 2 * W), F32),
             pltpu.VMEM((plan.lags, own, 2 * W), F32),
             pltpu.VMEM((C, M, 2 * W), F32),
-            pltpu.VMEM((2, plan.line, G, M, plan.cycles), BF16),
             pltpu.VMEM((2, plan.line * own, plan.ports), BF16),
-            pltpu.VMEM((plan.cycles, plan.ports), F32),
-            pltpu.VMEM((plan.cycles, plan.ports), BF16),
             dma((6,)), dma((N,)), dma((N,)), dma((plan.ways,)), dma((plan.ways,)),
-            dma((R + 1, G)), dma((R + 1, G)), dma((N, G * S, 4)), dma((N, G * S)), dma((C,)),
+            dma((R + 1, G)), dma((R + 1, G)), dma((N, G * S, 4)), dma((N, G * S)), dma,
         ],
         compiler_params=pltpu.CompilerParams(
             collective_id=0, has_side_effects=True, vmem_limit_bytes=LARGE_GRANT
         ),
+        name="response",
+    )(counters, signatures, eigen, taps, forward, inverse)
+
+
+def sag_kernel(plan, response, turned, sag, held, vectors, rounded, load_sem, store_sem):
+    W, C, modes = plan.width, plan.blocks, plan.port * plan.own
+    vectors_load = pltpu.make_async_copy(turned, vectors, load_sem.at[C])
+    loads = [
+        pltpu.make_async_copy(
+            response.at[:, :, :, :, pl.ds(a * W, W)], held.at[a], load_sem.at[a]
+        )
+        for a in range(C)
+    ]
+    loads[0].start()
+    vectors_load.start()
+    for load in loads[1:]:
+        load.start()
+    stores = []
+    for a in range(C):
+        loads[a].wait()
+        block = held[a].reshape(modes, W).T
+        if a == 0:
+            vectors_load.wait()
+        rows = pl.ds(a * W, W)
+        rounded[rows] = dot(block, vectors[...].reshape(modes, plan.ports)).astype(BF16)
+        stores.append(pltpu.make_async_copy(rounded.at[rows], sag.at[rows], store_sem.at[a]))
+        stores[a].start()
+    for store in stores:
+        store.wait()
+
+
+def sag_call(plan, response, turned):
+    line, G, M = plan.line, plan.groups, plan.group
+    return pl.pallas_call(
+        functools.partial(sag_kernel, plan),
+        out_shape=jax.ShapeDtypeStruct((plan.cycles, plan.ports), BF16),
+        in_specs=[pl.BlockSpec(memory_space=pl.ANY)] * 2,
+        out_specs=pl.BlockSpec(memory_space=pl.ANY),
+        scratch_shapes=[
+            pltpu.VMEM((plan.blocks, 2, line, G, M, plan.width), BF16),
+            pltpu.VMEM(turned.shape, BF16),
+            pltpu.VMEM((plan.cycles, plan.ports), BF16),
+            pltpu.SemaphoreType.DMA((plan.blocks + 1,)),
+            pltpu.SemaphoreType.DMA((plan.blocks,)),
+        ],
+        compiler_params=pltpu.CompilerParams(vmem_limit_bytes=LARGE_GRANT),
         name="sag",
-    )(counters, signatures, eigen, taps, forward, inverse)
+    )(response, turned)
 
 
 def solution(mesh):
@@ -431,9 +452,10 @@
             counters.shape[1], taps.shape[0], taps.shape[1],
         )
         forward, inverse = odd_dft(plan.width)
-        return sag_call(
+        response, turned = response_call(
             plan, counters, signatures, eigen, taps, jnp.asarray(forward), jnp.asarray(inverse)
         )
+        return sag_call(plan, response, turned)
 
     in_specs = (P("tm", None), P(None, "port"), P("port", None), P("port", None))
     return jax.shard_map(

time: 35.5 us -> 34.8 us (0.980)
  local copies, waits for them, and re-layouts: 3.08 us -> 0 us
  Pallas kernels: 32.3 us -> 34.6 us
    pallas_call x0 -> x1, Pallas kernels: none -> 31.4 us  [response_call(): pl.pallas_call(functools.partial(response_kernel, plan), out_shape=(jax.S...]
    pallas_call x1, Pallas kernels: 32.3 us -> 3.27 us  [sag_call(): pl.pallas_call(functools.partial(sag_kernel, plan), out_shape=jax.ShapeDt...]
    unnamed x1 -> x0, local copies, waits for them, and re-layouts: 3.08 us -> none
where the time goes in v6:
time: 34.8 us; the launch traced here: 34.6 us
  Pallas kernels  34.6 us (99%)
    pallas_call x1, Pallas kernels, response_call(): pl.pallas_call(functools.partial(response_kernel, plan), out_shape=(jax.S...  31.4 us
    pallas_call x1, Pallas kernels, sag_call(): pl.pallas_call(functools.partial(sag_kernel, plan), out_shape=jax.ShapeDt...  3.27 us

profile of v6, /device:TPU:2, one launch (start us, length us, event | category | flops | bytes accessed | tf_op | source)
XLA Modules:
  0.0 34.6 jit_solution(8587172074763644966)
XLA Ops:
  0.0 31.4 %response.1 = (bf16[2,4,2,16,1024]{4,3,2,1,0:T(8,128)(2,1)}, bf16[2,128,1024]{2,1,0:T(8,128)(2,1)}) custom-call(bf16[1024,256]{1,0:T(8,128)(2,1)} %counters.1, bf16[256,1024]{1,0:T(8,128)(2,1)} %signatures.1, bf16[1024,256]{1,0:T(8,128)(2,1)} %eigen.1, bf16[32,4096]{1,0:T(8,128)(2,1)} %taps.1, bf16[512,512]{1,0:T(8,128)(2,1)} %constant.4.clone.forward, ...), custom_call_target="tpu_custom_call" | custom-call | tf_op jit(solution)/shard_map/response/pallas_call | solution.py:369
  31.4 3.3 %sag.1 = bf16[1024,1024]{1,0:T(8,128)(2,1)} custom-call(bf16[2,4,2,16,1024]{4,3,2,1,0:T(8,128)(2,1)} %get-tuple-element.7.response, bf16[2,128,1024]{2,1,0:T(8,128)(2,1)} %get-tuple-element.8.turned), custom_call_target="tpu_custom_call" | custom-call | tf_op jit(solution)/shard_map/sag/pallas_call | solution.py:431

commit v7 on v6

--- a/solution.py
+++ b/solution.py
@@ -126,15 +126,8 @@
         taps_spectra[pl.ds(i * quad, quad)] = result.reshape(quad, own, 2 * W)
         return carry
 
-    lax.fori_loop(0, plan.lags // quad, taps_step, 0)
-    tile = min(256, plan.ports)
-    for i in range(plan.ports // tile):
-        block = eig[i * tile : (i + 1) * tile].T
-        for piece in range(N):
-            z, b = divmod(piece, 2)
-            turned[b, z * own : (z + 1) * own, i * tile : (i + 1) * tile] = block[piece * own : (piece + 1) * own]
-    turned_copy = pltpu.make_async_copy(turned, turned_out, turned_sem)
-    turned_copy.start()
+    steps = plan.lags // quad
+    lax.fori_loop(0, steps // 2, taps_step, 0)
     for d in range(1, R + 1):
         @pl.when(t < d)
         def _():
@@ -159,6 +152,7 @@
 
     for k in range(1, plan.ways):
         merged_copy(k).start()
+    lax.fori_loop(steps // 2, steps, taps_step, 0)
     loads[4].wait()
     for k in range(1, plan.ways):
         came = lax.rem(share + plan.ways - k, plan.ways)
@@ -187,6 +181,15 @@
             @pl.when(t + d < T)
             def _():
                 modal_copy(d, h).start()
+
+    tile = min(256, plan.ports)
+    for i in range(plan.ports // tile):
+        block = eig[i * tile : (i + 1) * tile].T
+        for piece in range(N):
+            z, b = divmod(piece, 2)
+            turned[b, z * own : (z + 1) * own, i * tile : (i + 1) * tile] = block[piece * own : (piece + 1) * own]
+    turned_copy = pltpu.make_async_copy(turned, turned_out, turned_sem)
+    turned_copy.start()
 
     sign = 1.0 - 2.0 * (lax.broadcasted_iota(jnp.int32, (8, 128), 1) % 2).astype(F32)
 

time: 34.8 us -> 34.8 us (level)
  no operation moved by 1% of the time
where the time goes in v7:
time: 34.8 us; the launch traced here: 34.6 us
  Pallas kernels  34.6 us (99%)
    pallas_call x1, Pallas kernels, response_call(): pl.pallas_call(functools.partial(response_kernel, plan), out_shape=(jax.S...  31.4 us
    pallas_call x1, Pallas kernels, sag_call(): pl.pallas_call(functools.partial(sag_kernel, plan), out_shape=jax.ShapeDt...  3.27 us

profile of v7, /device:TPU:2, one launch (start us, length us, event | category | flops | bytes accessed | tf_op | source)
XLA Modules:
  0.0 34.6 jit_solution(2803260931293610085)
XLA Ops:
  0.0 31.4 %response.1 = (bf16[2,4,2,16,1024]{4,3,2,1,0:T(8,128)(2,1)}, bf16[2,128,1024]{2,1,0:T(8,128)(2,1)}) custom-call(bf16[1024,256]{1,0:T(8,128)(2,1)} %counters.1, bf16[256,1024]{1,0:T(8,128)(2,1)} %signatures.1, bf16[1024,256]{1,0:T(8,128)(2,1)} %eigen.1, bf16[32,4096]{1,0:T(8,128)(2,1)} %taps.1, bf16[512,512]{1,0:T(8,128)(2,1)} %constant.4.clone.forward, ...), custom_call_target="tpu_custom_call" | custom-call | tf_op jit(solution)/shard_map/response/pallas_call | solution.py:372
  31.4 3.3 %sag.1 = bf16[1024,1024]{1,0:T(8,128)(2,1)} custom-call(bf16[2,4,2,16,1024]{4,3,2,1,0:T(8,128)(2,1)} %get-tuple-element.7.response, bf16[2,128,1024]{2,1,0:T(8,128)(2,1)} %get-tuple-element.8.turned), custom_call_target="tpu_custom_call" | custom-call | tf_op jit(solution)/shard_map/sag/pallas_call | solution.py:434
